TPU v7x, 512 devices: a whole 4x8x8 slice. The times are simulated.
512 devices in a mesh: expert: 64 (over x, z, core), replica: 8 (over y).
Axes of the slice: x: 4, y: 8, z: 8, core: 2. Of those that a mesh axis runs over, the one named last changes fastest.
Arguments:
- tokens: bfloat16 [768, 3584], P('expert', 'replica'), may hold values from -6 to 6
- expert_ids: int32 [768, 8], P('expert'), may hold values from 0 to 31, all different within a row; in each aligned block of 12 rows (0 to 11, 12 to 23, ...) at most 4 rows name the same one
- gate_values: float32 [768, 8], P('expert'), may hold values from 0.1 to 0.6
- gate_weight: bfloat16 [64, 512, 3584], P('expert', 'replica'), may hold values from -0.09375 to 0.09375
- up_weight: bfloat16 [64, 512, 3584], P('expert', 'replica'), may hold values from -0.09375 to 0.09375
- down_weight: bfloat16 [64, 512, 3584], P('expert', None, 'replica'), may hold values from -0.1875 to 0.1875
- out_grad: bfloat16 [768, 3584], P('expert', 'replica'), may hold values from -1.5 to 1.5
Outputs:
- moe_out: bfloat16 [768, 3584], P('expert', 'replica')
- token_grad: bfloat16 [768, 3584], P('expert', 'replica')
- gate_grad: bfloat16 [64, 512, 3584], P('expert', 'replica')
- up_grad: bfloat16 [64, 512, 3584], P('expert', 'replica')
- down_grad: bfloat16 [64, 512, 3584], P('expert', None, 'replica')
Inputs may be any that keep to these rules, and one draw needn't show every extreme that they name: `expert_ids`: each row names 8 different experts. Among the 12 rows of one index of expert, no expert is named by more than 4 rows, a bound that some block reaches.
All inputs are finite; a program needn't handle non-finite values.
Results may differ from a plain program's by a relative error of at most 0.0075.
Values may be sent and summed in bfloat16 or wider, within the bound.
A program may use at most 64 MiB of HBM per device.

v0:
```python
import jax
import jax.numpy as jnp
from jax import lax
from jax.sharding import PartitionSpec as P


def partner_2(block, axis, distance):
    count = lax.axis_size(axis)
    route = []
    for low in range(count):
        high = low | 1 << distance
        if high != low and high < count:
            route += [(low, high), (high, low)]
    return lax.ppermute(block, axis, route)


def pair_join(parity_bit, own_part, peer_part, stack_axis):
    first_part = jnp.where(parity_bit == 0, own_part, peer_part)
    second_part = jnp.where(parity_bit == 0, peer_part, own_part)
    return jnp.stack([first_part, second_part], axis=stack_axis)


def pick_half(parity_bit, stacked, stack_axis):
    lower = jnp.take(stacked, 0, axis=stack_axis)
    higher = jnp.take(stacked, 1, axis=stack_axis)
    return (jnp.where(parity_bit == 0, lower, higher), jnp.where(parity_bit == 0, higher, lower))


def per_device(tokens, expert_ids, gate_values, gate_weight, up_weight, down_weight, out_grad):
    experts_axis = lax.axis_size("expert")
    tok_rows, slice_width = tokens.shape
    top_count = expert_ids.shape[1]
    expert_count = experts_axis // 2
    most_rows = min(tok_rows, 4 * tok_rows * top_count // (3 * expert_count))
    capacity = (most_rows + 1) // 2
    pair_count = tok_rows * top_count
    slot_count = experts_axis * capacity
    flat_ids = expert_ids.reshape(pair_count)
    onehot = (flat_ids[:, None] == jnp.arange(expert_count, dtype=jnp.int32)[None, :]).astype(
        jnp.int32
    )
    rank_in = jnp.sum((jnp.cumsum(onehot, axis=0) - onehot) * onehot, axis=1)
    upper_copy = (rank_in >= capacity).astype(jnp.int32)
    target = (2 * flat_ids + upper_copy) * capacity + rank_in - upper_copy * capacity
    slot_match = target[None, :] == jnp.arange(slot_count, dtype=jnp.int32)[:, None]
    filled = jnp.any(slot_match, axis=1)
    source_pair = jnp.sum(
        jnp.where(slot_match, jnp.arange(pair_count, dtype=jnp.int32)[None, :], 0), axis=1
    )
    source_token = source_pair // top_count
    flat_gates = gate_values.reshape(pair_count)
    send_rows = jnp.where(filled[:, None], tokens[source_token], jnp.zeros((), tokens.dtype))
    scaled = flat_gates[source_pair][:, None] * out_grad[source_token].astype(jnp.float32)
    send_grads = jnp.where(filled[:, None], scaled, 0.0).astype(jnp.bfloat16)
    got_rows, got_grads = (
        lax.all_to_all(
            send_rows.reshape(experts_axis, capacity, slice_width),
            "expert",
            split_axis=0,
            concat_axis=0,
            tiled=True,
        ),
        lax.all_to_all(
            send_grads.reshape(experts_axis, capacity, slice_width),
            "expert",
            split_axis=0,
            concat_axis=0,
            tiled=True,
        ),
    )
    rows_part = got_rows.reshape(slot_count, slice_width)
    grads_part = got_grads.reshape(slot_count, slice_width)
    parity_bit = lax.axis_index("expert") % 2
    own_pieces = (gate_weight[0], up_weight[0], down_weight[0])
    partner = partner_2((own_pieces[0], own_pieces[1], own_pieces[2]), "expert", 0)
    w_gate = pair_join(parity_bit, own_pieces[0], partner[0], 0)
    w_up = pair_join(parity_bit, own_pieces[1], partner[1], 0)
    w_down = pair_join(parity_bit, own_pieces[2], partner[2], 0)
    _, quarter, model_width = w_gate.shape
    full_rows = lax.all_gather(rows_part, "replica", axis=1, tiled=True)
    contract = (((1,), (1,)), ((), ()))
    pre_gate = lax.dot_general(
        full_rows,
        w_gate.reshape(2 * quarter, model_width),
        contract,
        preferred_element_type=jnp.float32,
    ).reshape(slot_count, 2, quarter)
    pre_up = lax.dot_general(
        full_rows,
        w_up.reshape(2 * quarter, model_width),
        contract,
        preferred_element_type=jnp.float32,
    ).reshape(slot_count, 2, quarter)
    sigma = jax.nn.sigmoid(pre_gate)
    activated = pre_gate * sigma
    slope_term = sigma * (1.0 + pre_gate * (1.0 - sigma))
    hidden = (activated * pre_up).astype(jnp.bfloat16)
    all_hidden = lax.all_gather(hidden, "replica", axis=2, tiled=True).reshape(slot_count, -1)
    down_full = w_down.reshape(-1, slice_width)
    expert_out = jnp.dot(all_hidden, down_full, preferred_element_type=jnp.float32).astype(
        jnp.bfloat16
    )
    returned = lax.all_to_all(
        expert_out.reshape(experts_axis, capacity, slice_width),
        "expert",
        split_axis=0,
        concat_axis=0,
        tiled=True,
    ).reshape(slot_count, slice_width)
    picked = returned[target].astype(jnp.float32).reshape(tok_rows, top_count, slice_width)
    moe_out = jnp.sum(picked * gate_values[:, :, None], axis=1).astype(jnp.bfloat16)
    down_local = lax.dot_general(
        all_hidden, grads_part, (((0,), (0,)), ((), ())), preferred_element_type=jnp.float32
    )
    full_grads = lax.all_gather(grads_part, "replica", axis=1, tiled=True)
    down_rows = lax.all_to_all(w_down, "replica", split_axis=1, concat_axis=2, tiled=True)
    hidden_grad = jnp.einsum(
        "sd,hqd->shq", full_grads, down_rows, preferred_element_type=jnp.float32
    )
    gate_act = (hidden_grad * pre_up * slope_term).astype(jnp.bfloat16)
    up_act = (hidden_grad * activated).astype(jnp.bfloat16)
    gate_local = jnp.einsum("sd,shq->hqd", full_rows, gate_act, preferred_element_type=jnp.float32)
    up_local = jnp.einsum("sd,shq->hqd", full_rows, up_act, preferred_element_type=jnp.float32)
    all_gate_act, all_up_act = (
        lax.all_gather(gate_act, "replica", axis=2, tiled=True),
        lax.all_gather(up_act, "replica", axis=2, tiled=True),
    )
    rows_gate, rows_up = (
        lax.all_to_all(w_gate, "replica", split_axis=2, concat_axis=1, tiled=True),
        lax.all_to_all(w_up, "replica", split_axis=2, concat_axis=1, tiled=True),
    )
    input_rows = jnp.einsum(
        "shf,hfd->sd", all_gate_act, rows_gate, preferred_element_type=jnp.float32
    )
    input_rows = input_rows + jnp.einsum(
        "shf,hfd->sd", all_up_act, rows_up, preferred_element_type=jnp.float32
    )
    grads_back = lax.all_to_all(
        input_rows.astype(jnp.bfloat16).reshape(experts_axis, capacity, slice_width),
        "expert",
        split_axis=0,
        concat_axis=0,
        tiled=True,
    ).reshape(slot_count, slice_width)
    token_grad = jnp.sum(
        grads_back[target].astype(jnp.float32).reshape(tok_rows, top_count, slice_width), axis=1
    ).astype(jnp.bfloat16)
    keep_gate, give_gate = pick_half(parity_bit, gate_local, 0)
    keep_up, give_up = pick_half(parity_bit, up_local, 0)
    keep_down, give_down = pick_half(parity_bit, down_local.reshape(2, -1, slice_width), 0)
    received = (
        partner_2(give_gate.astype(jnp.bfloat16), "expert", 0).astype(give_gate.dtype),
        partner_2(give_up.astype(jnp.bfloat16), "expert", 0).astype(give_up.dtype),
        partner_2(give_down.astype(jnp.bfloat16), "expert", 0).astype(give_down.dtype),
    )
    gate_grad = (keep_gate + received[0]).astype(jnp.bfloat16)[None]
    up_grad = (keep_up + received[1]).astype(jnp.bfloat16)[None]
    down_grad = (keep_down + received[2]).astype(jnp.bfloat16)[None]
    return (moe_out, token_grad, gate_grad, up_grad, down_grad)


def solution(mesh):
    placed = (
        P("expert", "replica"),
        P("expert", None),
        P("expert", None),
        P("expert", "replica", None),
        P("expert", "replica", None),
        P("expert", None, "replica"),
        P("expert", "replica"),
    )
    return jax.shard_map(
        per_device,
        mesh=mesh,
        in_specs=placed,
        out_specs=(
            P("expert", "replica"),
            P("expert", "replica"),
            P("expert", "replica", None),
            P("expert", "replica", None),
            P("expert", None, "replica"),
        ),
        check_vma=False,
    )
```

profile of v0, /device:TPU:1, one launch (start us, length us, event | category | flops | bytes accessed | tf_op | source)
XLA Modules:
  0.0 322.7 jit_solution(3056633494185465903)
XLA Ops:
  0.7 8.9 %collective-permute-start.2 = (bf16[512,448]{0,1:T(8,128)(2,1)}, bf16[512,448]{0,1:T(8,128)(2,1)S(1)}, u32[]{:S(2)}, u32[]{:S(2)}) collective-permute-start(bf16[512,448]{0,1:T(8,128)(2,1)} %bitcast.169), channel_id=1, source_target_pairs={{0,8},{8,0},{16,24},{24,16},{32,40},{40,32},{48,56},{56,48},{64,72... | collective-permute-start | bytes 1376264 | tf_op jit(solution)/shard_map/ppermute | solution.py:14
  15.9 8.1 %all-to-all-start.2 = ((bf16[64,2,448]{2,1,0:T(2,128)(2,1)}), bf16[64,2,448]{2,1,0:T(2,128)(2,1)S(1)}, u32[]{:S(2)}, u32[]{:S(2)}) async-start(bf16[64,2,448]{2,1,0:T(2,128)(2,1)} %select_convert_fusion.3), calls=%async_computation.2 | async-start | bytes 262144 | tf_op jit(solution)/shard_map/all_to_all | solution.py:63
  24.0 2.4 collective-permute-start.1
  30.4 4.0 %all-to-all-done.2 = bf16[64,2,448]{2,1,0:T(2,128)(2,1)S(1)} async-done(((bf16[64,2,448]{2,1,0:T(2,128)(2,1)}), bf16[64,2,448]{2,1,0:T(2,128)(2,1)S(1)}, u32[]{:S(2)}, u32[]{:S(2)}) %all-to-all-start.2) | async-done | bytes 114720 | tf_op jit(solution)/shard_map/all_to_all | solution.py:63
  34.4 6.3 %all-to-all-start = ((bf16[64,2,448]{2,1,0:T(2,128)(2,1)}), bf16[64,2,448]{2,1,0:T(2,128)(2,1)S(1)}, u32[]{:S(2)}, u32[]{:S(2)}) async-start(bf16[64,2,448]{2,1,0:T(2,128)(2,1)} %broadcast_select_fusion), calls=%async_computation | async-start | bytes 262144 | tf_op jit(solution)/shard_map/all_to_all | solution.py:56
  41.6 9.5 %all-to-all-done = bf16[64,2,448]{2,1,0:T(2,128)(2,1)S(1)} async-done(((bf16[64,2,448]{2,1,0:T(2,128)(2,1)}), bf16[64,2,448]{2,1,0:T(2,128)(2,1)S(1)}, u32[]{:S(2)}, u32[]{:S(2)}) %all-to-all-start) | async-done | bytes 114720 | tf_op jit(solution)/shard_map/all_to_all | solution.py:56
  51.3 24.1 %all_gather.17 = bf16[128,3584]{0,1:T(8,128)(2,1)} all-gather(bf16[128,448]{0,1:T(8,128)(2,1)S(1)} %copy.62), channel_id=1, replica_groups=mesh['expert'=64,'replica'=8] {'replica'}, dimensions={1}, use_global_device_ids=true | all-gather | bytes 1032192 | tf_op jit(solution)/shard_map/all_gather | solution.py:115
  77.7 6.0 %all-to-all-start.3 = ((bf16[2,512,448]{2,0,1:T(2,128)(2,1)}), bf16[2,512,448]{2,0,1:T(2,128)(2,1)}, u32[]{:S(2)}, u32[]{:S(2)}) async-start(bf16[2,512,448]{2,0,1:T(2,128)(2,1)} %copy.63), calls=%async_computation.3 | async-start | bytes 2097152 | tf_op jit(solution)/shard_map/all_to_all | solution.py:116
  83.7 41.3 %all_gather.15 = bf16[128,3584]{0,1:T(8,128)(2,1)S(1)} all-gather(bf16[128,448]{0,1:T(8,128)(2,1)S(1)} %copy.57), channel_id=1, replica_groups=mesh['expert'=64,'replica'=8] {'replica'}, dimensions={1}, use_global_device_ids=true | all-gather | bytes 1032192 | tf_op jit(solution)/shard_map/all_gather | solution.py:80
  128.0 4.3 %copy.69 = bf16[2,64,3584]{1,0,2:T(2,128)(2,1)S(1)} copy(bf16[2,64,3584]{2,1,0:T(8,128)(2,1)} %pad_maximum_fusion.2) | data formatting | bytes 1835008 | tf_op jit(solution)/shard_map/stack | solution.py:20
  134.4 4.2 %all-to-all-start.5 = ((bf16[8,2,28672]{2,1,0:T(2,128)(2,1)}), bf16[8,2,28672]{2,1,0:T(2,128)(2,1)}, u32[]{:S(2)}, u32[]{:S(2)}) async-start(bf16[8,2,28672]{2,1,0:T(2,128)(2,1)} %reshape.363), calls=%async_computation.5 | async-start | bytes 1835008 | tf_op jit(solution)/shard_map/all_to_all | solution.py:130
  141.9 4.3 %copy.66 = bf16[2,64,3584]{1,0,2:T(2,128)(2,1)S(1)} copy(bf16[2,64,3584]{2,1,0:T(8,128)(2,1)} %pad_maximum_fusion.1) | data formatting | bytes 1835008 | tf_op jit(solution)/shard_map/stack | solution.py:20
  154.5 6.7 %all-to-all-start.4 = ((bf16[8,2,28672]{2,1,0:T(2,128)(2,1)}), bf16[8,2,28672]{2,1,0:T(2,128)(2,1)}, u32[]{:S(2)}, u32[]{:S(2)}) async-start(bf16[8,2,28672]{2,1,0:T(2,128)(2,1)} %reshape.365), calls=%async_computation.4 | async-start | bytes 1835008 | tf_op jit(solution)/shard_map/all_to_all | solution.py:129
  162.8 30.9 %all_gather.16 = bf16[128,2,512]{0,2,1:T(8,128)(2,1)S(1)} all-gather(bf16[128,2,64]{0,2,1:T(8,128)(2,1)S(1)} %get-tuple-element.61), channel_id=1, replica_groups=mesh['expert'=64,'replica'=8] {'replica'}, dimensions={2}, use_global_device_ids=true | all-gather | bytes 294912 | tf_op jit(solution)/shard_map/all_gather | solution.py:98
  195.1 4.5 %reshape.364 = bf16[3584,2,64]{2,1,0:T(2,128)(2,1)S(1)} reshape(bf16[8,2,28672]{2,1,0:T(2,128)(2,1)} %all-to-all-done.5) | data formatting | bytes 1835008
  199.6 3.5 %copy.70 = bf16[2,64,8,448]{3,1,2,0:T(8,128)(2,1)} copy(bf16[2,64,8,448]{1,0,3,2:T(2,128)(2,1)S(1)} %bitcast.164) | data formatting | bytes 1835008 | tf_op jit(solution)/shard_map/all_to_all | solution.py:130
  203.1 18.4 %all_gather.19 = bf16[128,2,512]{0,2,1:T(8,128)(2,1)S(1)} all-gather(bf16[128,2,64]{0,2,1:T(8,128)(2,1)S(1)} %get-tuple-element.60), channel_id=1, replica_groups=mesh['expert'=64,'replica'=8] {'replica'}, dimensions={2}, use_global_device_ids=true | all-gather | bytes 294912 | tf_op jit(solution)/shard_map/all_gather | solution.py:126
  221.5 18.8 %all_gather.18 = bf16[128,2,512]{0,2,1:T(8,128)(2,1)S(1)} all-gather(bf16[128,2,64]{0,2,1:T(8,128)(2,1)S(1)} %get-tuple-element.59), channel_id=1, replica_groups=mesh['expert'=64,'replica'=8] {'replica'}, dimensions={2}, use_global_device_ids=true | all-gather | bytes 294912 | tf_op jit(solution)/shard_map/all_gather | solution.py:125
  242.3 27.9 %all-to-all-start.1 = ((bf16[64,2,448]{2,1,0:T(2,128)(2,1)}), bf16[64,2,448]{2,1,0:T(2,128)(2,1)S(1)}, u32[]{:S(2)}, u32[]{:S(2)}) async-start(bf16[64,2,448]{2,1,0:T(2,128)(2,1)} %reshape.212), calls=%async_computation.1 | async-start | bytes 262144 | tf_op jit(solution)/shard_map/all_to_all | solution.py:103
  270.2 5.3 %reshape.366 = bf16[3584,2,64]{2,1,0:T(2,128)(2,1)} reshape(bf16[8,2,28672]{2,1,0:T(2,128)(2,1)} %all-to-all-done.4) | data formatting | bytes 1835008
  275.5 5.8 %copy.67 = bf16[2,64,8,448]{3,1,2,0:T(8,128)(2,1)} copy(bf16[2,64,8,448]{1,0,3,2:T(2,128)(2,1)} %bitcast.165) | data formatting | bytes 1835008 | tf_op jit(solution)/shard_map/all_to_all | solution.py:129
  293.0 10.3 %all-to-all-start.6 = ((bf16[64,2,448]{2,1,0:T(2,128)(2,1)}), bf16[64,2,448]{2,1,0:T(2,128)(2,1)S(1)}, u32[]{:S(2)}, u32[]{:S(2)}) async-start(bf16[64,2,448]{2,1,0:T(2,128)(2,1)} %reshape.216), calls=%async_computation.6 | async-start | bytes 262144 | tf_op jit(solution)/shard_map/all_to_all | solution.py:138
  308.2 5.4 %all-to-all-done.6 = bf16[64,2,448]{2,1,0:T(2,128)(2,1)S(1)} async-done(((bf16[64,2,448]{2,1,0:T(2,128)(2,1)}), bf16[64,2,448]{2,1,0:T(2,128)(2,1)S(1)}, u32[]{:S(2)}, u32[]{:S(2)}) %all-to-all-start.6) | async-done | bytes 114720 | tf_op jit(solution)/shard_map/all_to_all | solution.py:138
  316.1 2.5 fusion.13
  (124 shorter events, 58.2 us)
Async XLA Ops:
  0.6 10.5 %copy-start = (bf16[12,448]{1,0:T(8,128)(2,1)S(1)}, bf16[12,448]{1,0:T(8,128)(2,1)}, u32[]{:S(2)}) copy-start(bf16[12,448]{1,0:T(8,128)(2,1)} %param.21) | copy-start | bytes 32260
  0.6 27.7 %copy-start.20 = (s32[12,8]{0,1:T(8,128)S(1)}, s32[12,8]{0,1:T(8,128)}, u32[]{:S(2)}) copy-start(s32[12,8]{0,1:T(8,128)} %param.16) | copy-start | bytes 1156
  0.7 23.4 %copy-start.17 = (bf16[1,64,3584]{2,1,0:T(8,128)(2,1)S(1)}, bf16[1,64,3584]{2,1,0:T(8,128)(2,1)}, u32[]{:S(2)}) copy-start(bf16[1,64,3584]{2,1,0:T(8,128)(2,1)} %param.19) | copy-start | bytes 1376260
  0.7 27.7 %copy-start.1 = (bf16[12,448]{1,0:T(8,128)(2,1)S(1)}, bf16[12,448]{1,0:T(8,128)(2,1)}, u32[]{:S(2)}) copy-start(bf16[12,448]{1,0:T(8,128)(2,1)} %param.15) | copy-start | bytes 32260
  0.7 74.7 %collective-permute-start.2 = (bf16[512,448]{0,1:T(8,128)(2,1)}, bf16[512,448]{0,1:T(8,128)(2,1)S(1)}, u32[]{:S(2)}, u32[]{:S(2)}) collective-permute-start(bf16[512,448]{0,1:T(8,128)(2,1)} %bitcast.169), channel_id=1, source_target_pairs={{0,8},{8,0},{16,24},{24,16},{32,40},{40,32},{48,56},{56,48},{64,72... | collective-permute-start | bytes 1376264 | tf_op jit(solution)/shard_map/ppermute | solution.py:14
  15.9 18.4 %all-to-all-start.2 = ((bf16[64,2,448]{2,1,0:T(2,128)(2,1)}), bf16[64,2,448]{2,1,0:T(2,128)(2,1)S(1)}, u32[]{:S(2)}, u32[]{:S(2)}) async-start(bf16[64,2,448]{2,1,0:T(2,128)(2,1)} %select_convert_fusion.3), calls=%async_computation.2 | async-start | bytes 262144 | tf_op jit(solution)/shard_map/all_to_all | solution.py:63
  24.0 101.0 %collective-permute-start.1 = (bf16[64,3584]{1,0:T(8,128)(2,1)S(1)}, bf16[64,3584]{1,0:T(8,128)(2,1)}, u32[]{:S(2)}, u32[]{:S(2)}) collective-permute-start(bf16[64,3584]{1,0:T(8,128)(2,1)S(1)} %bitcast.170), channel_id=1, source_target_pairs={{0,8},{8,0},{16,24},{24,16},{32,40},{40,32},{48,56},{56,48},{64,72... | collective-permute-start | bytes 1376264 | tf_op jit(solution)/shard_map/ppermute | solution.py:14
  26.4 112.3 %collective-permute-start = (bf16[64,3584]{1,0:T(8,128)(2,1)}, bf16[64,3584]{1,0:T(8,128)(2,1)}, u32[]{:S(2)}, u32[]{:S(2)}) collective-permute-start(bf16[64,3584]{1,0:T(8,128)(2,1)} %bitcast.3), channel_id=1, source_target_pairs={{0,8},{8,0},{16,24},{24,16},{32,40},{40,32},{48,56},{56,48},{64,72... | collective-permute-start | bytes 1376264 | tf_op jit(solution)/shard_map/ppermute | solution.py:14
  28.4 47.0 %copy-start.16 = (bf16[1,512,448]{1,2,0:T(8,128)(2,1)S(1)}, bf16[1,512,448]{1,2,0:T(8,128)(2,1)}, u32[]{:S(2)}) copy-start(bf16[1,512,448]{1,2,0:T(8,128)(2,1)} %param.20) | copy-start | bytes 1376260
  34.4 16.7 %all-to-all-start = ((bf16[64,2,448]{2,1,0:T(2,128)(2,1)}), bf16[64,2,448]{2,1,0:T(2,128)(2,1)S(1)}, u32[]{:S(2)}, u32[]{:S(2)}) async-start(bf16[64,2,448]{2,1,0:T(2,128)(2,1)} %broadcast_select_fusion), calls=%async_computation | async-start | bytes 262144 | tf_op jit(solution)/shard_map/all_to_all | solution.py:56
  77.7 56.7 %all-to-all-start.3 = ((bf16[2,512,448]{2,0,1:T(2,128)(2,1)}), bf16[2,512,448]{2,0,1:T(2,128)(2,1)}, u32[]{:S(2)}, u32[]{:S(2)}) async-start(bf16[2,512,448]{2,0,1:T(2,128)(2,1)} %copy.63), calls=%async_computation.3 | async-start | bytes 2097152 | tf_op jit(solution)/shard_map/all_to_all | solution.py:116
  134.4 20.1 %all-to-all-start.5 = ((bf16[8,2,28672]{2,1,0:T(2,128)(2,1)}), bf16[8,2,28672]{2,1,0:T(2,128)(2,1)}, u32[]{:S(2)}, u32[]{:S(2)}) async-start(bf16[8,2,28672]{2,1,0:T(2,128)(2,1)} %reshape.363), calls=%async_computation.5 | async-start | bytes 1835008 | tf_op jit(solution)/shard_map/all_to_all | solution.py:130
  152.4 8.8 %copy-start.4 = (bf16[128,3584]{0,1:T(8,128)(2,1)S(1)}, bf16[128,3584]{0,1:T(8,128)(2,1)}, u32[]{:S(2)}) copy-start(bf16[128,3584]{0,1:T(8,128)(2,1)} %all_gather.17) | copy-start | bytes 2752516
  154.5 6.7 %copy-start.5 = (bf16[2,64,3584]{2,1,0:T(8,128)(2,1)S(1)}, bf16[2,64,3584]{2,1,0:T(8,128)(2,1)}, u32[]{:S(2)}) copy-start(bf16[2,64,3584]{2,1,0:T(8,128)(2,1)} %all_to_all.57) | copy-start | bytes 2752516
  154.5 7.1 %copy-start.21 = (f32[128,2,64]{0,2,1:T(8,128)S(1)}, f32[128,2,64]{0,2,1:T(8,128)}, u32[]{:S(2)}) copy-start(f32[128,2,64]{0,2,1:T(8,128)} %fusion.9) | copy-start | bytes 196612
  154.5 87.8 %all-to-all-start.4 = ((bf16[8,2,28672]{2,1,0:T(2,128)(2,1)}), bf16[8,2,28672]{2,1,0:T(2,128)(2,1)}, u32[]{:S(2)}, u32[]{:S(2)}) async-start(bf16[8,2,28672]{2,1,0:T(2,128)(2,1)} %reshape.365), calls=%async_computation.4 | async-start | bytes 1835008 | tf_op jit(solution)/shard_map/all_to_all | solution.py:129
  162.3 31.3 %copy-start.7 = (bf16[1,512,448]{1,2,0:T(8,128)(2,1)S(1)}, bf16[1,512,448]{1,2,0:T(8,128)(2,1)}, u32[]{:S(2)}) copy-start(bf16[1,512,448]{1,2,0:T(8,128)(2,1)} %copy-done.6) | copy-start | bytes 1376260
  242.3 50.6 %all-to-all-start.1 = ((bf16[64,2,448]{2,1,0:T(2,128)(2,1)}), bf16[64,2,448]{2,1,0:T(2,128)(2,1)S(1)}, u32[]{:S(2)}, u32[]{:S(2)}) async-start(bf16[64,2,448]{2,1,0:T(2,128)(2,1)} %reshape.212), calls=%async_computation.1 | async-start | bytes 262144 | tf_op jit(solution)/shard_map/all_to_all | solution.py:103
  283.7 7.6 %copy-start.15 = (bf16[128,2,512]{0,2,1:T(8,128)(2,1)S(1)}, bf16[128,2,512]{0,2,1:T(8,128)(2,1)}, u32[]{:S(2)}) copy-start(bf16[128,2,512]{0,2,1:T(8,128)(2,1)} %copy-done.14) | copy-start | bytes 786436
  286.9 29.2 %collective-permute-start.3 = (bf16[64,3584]{1,0:T(8,128)(2,1)}, bf16[64,3584]{1,0:T(8,128)(2,1)}, u32[]{:S(2)}, u32[]{:S(2)}) collective-permute-start(bf16[64,3584]{1,0:T(8,128)(2,1)} %select_convert_fusion.2), channel_id=1, source_target_pairs={{0,8},{8,0},{16,24},{24,16},{32,40},{40,32},{48,56},{56,48},{64,72... | collective-permute-start | bytes 1376264 | tf_op jit(solution)/shard_map/ppermute | solution.py:14
  289.3 29.2 %collective-permute-start.4 = (bf16[64,3584]{1,0:T(8,128)(2,1)S(1)}, bf16[64,3584]{1,0:T(8,128)(2,1)}, u32[]{:S(2)}, u32[]{:S(2)}) collective-permute-start(bf16[64,3584]{1,0:T(8,128)(2,1)S(1)} %select_convert_fusion.1), channel_id=1, source_target_pairs={{0,8},{8,0},{16,24},{24,16},{32,40},{40,32},{48,56},{56,48},{64,72... | collective-permute-start | bytes 1376264 | tf_op jit(solution)/shard_map/ppermute | solution.py:14
  293.0 20.7 %all-to-all-start.6 = ((bf16[64,2,448]{2,1,0:T(2,128)(2,1)}), bf16[64,2,448]{2,1,0:T(2,128)(2,1)S(1)}, u32[]{:S(2)}, u32[]{:S(2)}) async-start(bf16[64,2,448]{2,1,0:T(2,128)(2,1)} %reshape.216), calls=%async_computation.6 | async-start | bytes 262144 | tf_op jit(solution)/shard_map/all_to_all | solution.py:138
  303.3 12.1 %copy-start.19 = (f32[12,8]{1,0:T(8,128)S(1)}, f32[12,8]{1,0:T(8,128)}, u32[]{:S(2)}) copy-start(f32[12,8]{1,0:T(8,128)} %copy-done.18) | copy-start | bytes 1156
  304.8 15.7 %collective-permute-start.5 = (bf16[512,448]{0,1:T(8,128)(2,1)S(1)}, bf16[512,448]{0,1:T(8,128)(2,1)}, u32[]{:S(2)}, u32[]{:S(2)}) collective-permute-start(bf16[512,448]{0,1:T(8,128)(2,1)S(1)} %select_convert_fusion), channel_id=1, source_target_pairs={{0,8},{8,0},{16,24},{24,16},{32,40},{40,32},{48,56},{56,48},{64,72... | collective-permute-start | bytes 1376264 | tf_op jit(solution)/shard_map/ppermute | solution.py:14
  (11 other events, 13.0 us)
where the time goes:
time: 324 us; the launch traced here: 323 us
  blocking collectives  133 us (41%)
  starting transfers between devices  89.4 us (28%)
  local copies, waits for them, and re-layouts  50.9 us (16%)
  other arithmetic  19.4 us (6%)
  waiting for transfers between devices  18.9 us (6%)
  matrix products  9.43 us (3%)
    all_gather x1, blocking collectives, per_device(): full_rows = lax.all_gather(rows_part, 'replica', axis=1, tiled=True)  41.3 us
    all_gather x1, blocking collectives, per_device(): lax.all_gather(hidden, 'replica', axis=2, tiled=True)  30.9 us
    all_to_all x1, starting transfers between devices, per_device(): lax.all_to_all(expert_out.reshape(experts_axis, capacity, slice_width), '...  27.9 us
    all_gather x1, blocking collectives, per_device(): full_grads = lax.all_gather(grads_part, 'replica', axis=1, tiled=True)  24.1 us
    ppermute x6, starting transfers between devices, partner_2(): return lax.ppermute(block, axis, route)  19.9 us
    unnamed x50, local copies, waits for them, and re-layouts  18.8 us
    all_gather x1, blocking collectives, per_device(): lax.all_gather(gate_act, 'replica', axis=2, tiled=True)  18.8 us
    all_gather x1, blocking collectives, per_device(): lax.all_gather(up_act, 'replica', axis=2, tiled=True)  18.4 us
  transfers between devices with their start and end apart: 13, of which 3 were waited for; matrix products, arithmetic and copies ran while one was open for 22% of the time, Pallas kernels for 0%

commit v1 on v0

--- a/solution.py
+++ b/solution.py
@@ -2,6 +2,10 @@
 import jax.numpy as jnp
 from jax import lax
 from jax.sharding import PartitionSpec as P
+
+divide_heaps_by_axis = lambda local_values: jnp.concatenate(
+    lax.all_to_all(jnp.stack(lax.psum(1, "replica") * [local_values], 0), "replica", 0, 0), 2
+)
 
 
 def partner_2(block, axis, distance):
@@ -122,7 +126,7 @@
     gate_local = jnp.einsum("sd,shq->hqd", full_rows, gate_act, preferred_element_type=jnp.float32)
     up_local = jnp.einsum("sd,shq->hqd", full_rows, up_act, preferred_element_type=jnp.float32)
     all_gate_act, all_up_act = (
-        lax.all_gather(gate_act, "replica", axis=2, tiled=True),
+        divide_heaps_by_axis(gate_act),
         lax.all_gather(up_act, "replica", axis=2, tiled=True),
     )
     rows_gate, rows_up = (

time: 324 us -> 314 us (0.969)
  blocking collectives: 133 us -> 117 us
  waiting for transfers between devices: 18.9 us -> 26.4 us
  starting transfers between devices: 89.4 us -> 82.2 us
  local copies, waits for them, and re-layouts: 50.9 us -> 56.2 us
    all_to_all x1, starting transfers between devices: 27.9 us -> 4.89 us  [per_device(): lax.all_to_all(expert_out.reshape(experts_axis, capacity, slice_width), '...]
    all_gather x1 -> x0, blocking collectives: 18.8 us -> none  [per_device(): lax.all_gather(gate_act, 'replica', axis=2, tiled=True)]
    ppermute x6, starting transfers between devices: 19.9 us -> 30.7 us  [partner_2(): return lax.ppermute(block, axis, route)]
    all_to_all x1, waiting for transfers between devices: 0.01 us -> 8.68 us  [per_device(): lax.all_to_all(expert_out.reshape(experts_axis, capacity, slice_width), '...]
    all_to_all x0 -> x1, starting transfers between devices: none -> 4.91 us  [lax.all_to_all(jnp.stack(lax.psum(1, 'replica') * [local_values], 0), 're...]
    unnamed x50 -> x46, local copies, waits for them, and re-layouts: 18.8 us -> 20.7 us
  transfers between devices with their start and end apart: 13 -> 14, of which waited for: 3 -> 4; matrix products, arithmetic and copies ran while one was open for 22% -> 25% of each run, Pallas kernels for 0% -> 0%
where the time goes in v1:
time: 314 us; the launch traced here: 312 us
  blocking collectives  117 us (37%)
  starting transfers between devices  82.2 us (26%)
  local copies, waits for them, and re-layouts  56.2 us (18%)
  waiting for transfers between devices  26.4 us (8%)
  other arithmetic  20.1 us (6%)
  matrix products  8.77 us (3%)
    all_gather x1, blocking collectives, per_device(): full_rows = lax.all_gather(rows_part, 'replica', axis=1, tiled=True)  41.3 us
    all_gather x1, blocking collectives, per_device(): lax.all_gather(hidden, 'replica', axis=2, tiled=True)  31.6 us
    ppermute x6, starting transfers between devices, partner_2(): return lax.ppermute(block, axis, route)  30.7 us
    all_gather x1, blocking collectives, per_device(): full_grads = lax.all_gather(grads_part, 'replica', axis=1, tiled=True)  24.1 us
    unnamed x46, local copies, waits for them, and re-layouts  20.7 us
    all_gather x1, blocking collectives, per_device(): lax.all_gather(up_act, 'replica', axis=2, tiled=True)  20.3 us
    another operation x3, local copies, waits for them, and re-layouts, pair_join(): return jnp.stack([first_part, second_part], axis=stack_axis)  10.7 us
    all_to_all x1, starting transfers between devices, per_device(): lax.all_to_all(input_rows.astype(jnp.bfloat16).reshape(experts_axis, capa...  10.5 us
  transfers between devices with their start and end apart: 14, of which 4 were waited for; matrix products, arithmetic and copies ran while one was open for 25% of the time, Pallas kernels for 0%

profile of v1, /device:TPU:1, one launch (start us, length us, event | category | flops | bytes accessed | tf_op | source)
XLA Modules:
  0.0 312.1 jit_solution(4653211412755513477)
XLA Ops:
  0.7 8.9 %collective-permute-start.2 = (bf16[512,448]{0,1:T(8,128)(2,1)}, bf16[512,448]{0,1:T(8,128)(2,1)S(1)}, u32[]{:S(2)}, u32[]{:S(2)}) collective-permute-start(bf16[512,448]{0,1:T(8,128)(2,1)} %bitcast.173), channel_id=1, source_target_pairs={{0,8},{8,0},{16,24},{24,16},{32,40},{40,32},{48,56},{56,48},{64,72... | collective-permute-start | bytes 1376264 | tf_op jit(solution)/shard_map/ppermute | solution.py:18
  15.9 8.1 %all-to-all-start.2 = ((bf16[64,2,448]{2,1,0:T(2,128)(2,1)}), bf16[64,2,448]{2,1,0:T(2,128)(2,1)S(1)}, u32[]{:S(2)}, u32[]{:S(2)}) async-start(bf16[64,2,448]{2,1,0:T(2,128)(2,1)} %select_convert_fusion.3), calls=%async_computation.2 | async-start | bytes 262144 | tf_op jit(solution)/shard_map/all_to_all | solution.py:67
  30.4 4.0 %all-to-all-done.2 = bf16[64,2,448]{2,1,0:T(2,128)(2,1)S(1)} async-done(((bf16[64,2,448]{2,1,0:T(2,128)(2,1)}), bf16[64,2,448]{2,1,0:T(2,128)(2,1)S(1)}, u32[]{:S(2)}, u32[]{:S(2)}) %all-to-all-start.2) | async-done | bytes 114720 | tf_op jit(solution)/shard_map/all_to_all | solution.py:67
  34.4 6.3 %all-to-all-start = ((bf16[64,2,448]{2,1,0:T(2,128)(2,1)}), bf16[64,2,448]{2,1,0:T(2,128)(2,1)S(1)}, u32[]{:S(2)}, u32[]{:S(2)}) async-start(bf16[64,2,448]{2,1,0:T(2,128)(2,1)} %broadcast_select_fusion), calls=%async_computation | async-start | bytes 262144 | tf_op jit(solution)/shard_map/all_to_all | solution.py:60
  41.6 9.5 %all-to-all-done = bf16[64,2,448]{2,1,0:T(2,128)(2,1)S(1)} async-done(((bf16[64,2,448]{2,1,0:T(2,128)(2,1)}), bf16[64,2,448]{2,1,0:T(2,128)(2,1)S(1)}, u32[]{:S(2)}, u32[]{:S(2)}) %all-to-all-start) | async-done | bytes 114720 | tf_op jit(solution)/shard_map/all_to_all | solution.py:60
  51.3 24.1 %all_gather.14 = bf16[128,3584]{0,1:T(8,128)(2,1)} all-gather(bf16[128,448]{0,1:T(8,128)(2,1)S(1)} %copy.66), channel_id=1, replica_groups=mesh['expert'=64,'replica'=8] {'replica'}, dimensions={1}, use_global_device_ids=true | all-gather | bytes 1032192 | tf_op jit(solution)/shard_map/all_gather | solution.py:119
  77.7 6.0 %all-to-all-start.3 = ((bf16[2,512,448]{2,0,1:T(2,128)(2,1)}), bf16[2,512,448]{2,0,1:T(2,128)(2,1)}, u32[]{:S(2)}, u32[]{:S(2)}) async-start(bf16[2,512,448]{2,0,1:T(2,128)(2,1)} %copy.67), calls=%async_computation.3 | async-start | bytes 2097152 | tf_op jit(solution)/shard_map/all_to_all | solution.py:120
  83.7 41.3 %all_gather.12 = bf16[128,3584]{0,1:T(8,128)(2,1)S(1)} all-gather(bf16[128,448]{0,1:T(8,128)(2,1)S(1)} %copy.61), channel_id=1, replica_groups=mesh['expert'=64,'replica'=8] {'replica'}, dimensions={1}, use_global_device_ids=true | all-gather | bytes 1032192 | tf_op jit(solution)/shard_map/all_gather | solution.py:84
  128.1 4.3 %copy.75 = bf16[2,64,3584]{1,0,2:T(2,128)(2,1)S(1)} copy(bf16[2,64,3584]{2,1,0:T(8,128)(2,1)} %pad_maximum_fusion.2) | data formatting | bytes 1835008 | tf_op jit(solution)/shard_map/stack | solution.py:24
  134.5 4.2 %all-to-all-start.6 = ((bf16[8,2,28672]{2,1,0:T(2,128)(2,1)}), bf16[8,2,28672]{2,1,0:T(2,128)(2,1)}, u32[]{:S(2)}, u32[]{:S(2)}) async-start(bf16[8,2,28672]{2,1,0:T(2,128)(2,1)} %reshape.373), calls=%async_computation.6 | async-start | bytes 1835008 | tf_op jit(solution)/shard_map/all_to_all | solution.py:134
  141.9 4.3 %copy.71 = bf16[2,64,3584]{1,0,2:T(2,128)(2,1)S(1)} copy(bf16[2,64,3584]{2,1,0:T(8,128)(2,1)} %pad_maximum_fusion.1) | data formatting | bytes 1835008 | tf_op jit(solution)/shard_map/stack | solution.py:24
  156.8 6.5 %all-to-all-start.5 = ((bf16[8,2,28672]{2,1,0:T(2,128)(2,1)}), bf16[8,2,28672]{2,1,0:T(2,128)(2,1)}, u32[]{:S(2)}, u32[]{:S(2)}) async-start(bf16[8,2,28672]{2,1,0:T(2,128)(2,1)} %reshape.375), calls=%async_computation.5 | async-start | bytes 1835008 | tf_op jit(solution)/shard_map/all_to_all | solution.py:133
  164.2 31.6 %all_gather.13 = bf16[128,2,512]{0,2,1:T(8,128)(2,1)S(1)} all-gather(bf16[128,2,64]{0,2,1:T(8,128)(2,1)S(1)} %get-tuple-element.61), channel_id=1, replica_groups=mesh['expert'=64,'replica'=8] {'replica'}, dimensions={2}, use_global_device_ids=true | all-gather | bytes 294912 | tf_op jit(solution)/shard_map/all_gather | solution.py:102
  198.8 5.3 %reshape.374 = bf16[3584,2,64]{2,1,0:T(2,128)(2,1)} reshape(bf16[8,2,28672]{2,1,0:T(2,128)(2,1)} %all-to-all-done.6) | data formatting | bytes 1835008
  204.1 5.9 %copy.76 = bf16[2,64,8,448]{3,1,2,0:T(8,128)(2,1)} copy(bf16[2,64,8,448]{1,0,3,2:T(2,128)(2,1)} %bitcast.167) | data formatting | bytes 1835008 | tf_op jit(solution)/shard_map/all_to_all | solution.py:134
  209.9 13.0 %collective-permute-start.3 = (bf16[64,3584]{1,0:T(8,128)(2,1)}, bf16[64,3584]{1,0:T(8,128)(2,1)}, u32[]{:S(2)}, u32[]{:S(2)}) collective-permute-start(bf16[64,3584]{1,0:T(8,128)(2,1)} %select_convert_fusion.2), channel_id=1, source_target_pairs={{0,8},{8,0},{16,24},{24,16},{32,40},{40,32},{48,56},{56,48},{64,72... | collective-permute-start | bytes 1376264 | tf_op jit(solution)/shard_map/ppermute | solution.py:18
  227.4 4.9 %all-to-all-start.1 = ((bf16[64,2,448]{2,1,0:T(2,128)(2,1)}), bf16[64,2,448]{2,1,0:T(2,128)(2,1)S(1)}, u32[]{:S(2)}, u32[]{:S(2)}) async-start(bf16[64,2,448]{2,1,0:T(2,128)(2,1)} %reshape.220), calls=%async_computation.1 | async-start | bytes 262144 | tf_op jit(solution)/shard_map/all_to_all | solution.py:107
  234.0 8.7 %all-to-all-done.1 = bf16[64,2,448]{2,1,0:T(2,128)(2,1)S(1)} async-done(((bf16[64,2,448]{2,1,0:T(2,128)(2,1)}), bf16[64,2,448]{2,1,0:T(2,128)(2,1)S(1)}, u32[]{:S(2)}, u32[]{:S(2)}) %all-to-all-start.1) | async-done | bytes 114720 | tf_op jit(solution)/shard_map/all_to_all | solution.py:107
  243.4 4.9 %all-to-all-start.4 = ((bf16[8,128,2,64]{1,3,2,0:T(8,128)(2,1)}), bf16[8,128,2,64]{1,3,2,0:T(8,128)(2,1)S(1)}, u32[]{:S(2)}, u32[]{:S(2)}) async-start(bf16[8,128,2,64]{1,3,2,0:T(8,128)(2,1)} %stack.47), calls=%async_computation.4 | async-start | bytes 524288 | tf_op jit(solution)/shard_map/all_to_all | solution.py:7
  253.2 20.3 %all_gather.15 = bf16[128,2,512]{0,2,1:T(8,128)(2,1)S(1)} all-gather(bf16[128,2,64]{0,2,1:T(8,128)(2,1)S(1)} %get-tuple-element.60), channel_id=1, replica_groups=mesh['expert'=64,'replica'=8] {'replica'}, dimensions={2}, use_global_device_ids=true | all-gather | bytes 294912 | tf_op jit(solution)/shard_map/all_gather | solution.py:130
  274.1 5.3 %reshape.376 = bf16[3584,2,64]{2,1,0:T(2,128)(2,1)} reshape(bf16[8,2,28672]{2,1,0:T(2,128)(2,1)} %all-to-all-done.5) | data formatting | bytes 1835008
  279.4 4.6 %copy.72 = bf16[2,64,8,448]{3,1,2,0:T(8,128)(2,1)S(1)} copy(bf16[2,64,8,448]{1,0,3,2:T(2,128)(2,1)} %bitcast.168) | data formatting | bytes 1835008 | tf_op jit(solution)/shard_map/all_to_all | solution.py:133
  289.6 10.5 %all-to-all-start.7 = ((bf16[64,2,448]{2,1,0:T(2,128)(2,1)}), bf16[64,2,448]{2,1,0:T(2,128)(2,1)S(1)}, u32[]{:S(2)}, u32[]{:S(2)}) async-start(bf16[64,2,448]{2,1,0:T(2,128)(2,1)} %reshape.226), calls=%async_computation.7 | async-start | bytes 262144 | tf_op jit(solution)/shard_map/all_to_all | solution.py:142
  306.3 4.2 %all-to-all-done.7 = bf16[64,2,448]{2,1,0:T(2,128)(2,1)S(1)} async-done(((bf16[64,2,448]{2,1,0:T(2,128)(2,1)}), bf16[64,2,448]{2,1,0:T(2,128)(2,1)S(1)}, u32[]{:S(2)}, u32[]{:S(2)}) %all-to-all-start.7) | async-done | bytes 114720 | tf_op jit(solution)/shard_map/all_to_all | solution.py:142
  (123 shorter events, 64.2 us)
Async XLA Ops:
  0.6 10.5 %copy-start = (bf16[12,448]{1,0:T(8,128)(2,1)S(1)}, bf16[12,448]{1,0:T(8,128)(2,1)}, u32[]{:S(2)}) copy-start(bf16[12,448]{1,0:T(8,128)(2,1)} %param.21) | copy-start | bytes 32260
  0.6 27.7 %copy-start.19 = (s32[12,8]{0,1:T(8,128)S(1)}, s32[12,8]{0,1:T(8,128)}, u32[]{:S(2)}) copy-start(s32[12,8]{0,1:T(8,128)} %param.16) | copy-start | bytes 1156
  0.7 27.7 %copy-start.1 = (bf16[12,448]{1,0:T(8,128)(2,1)S(1)}, bf16[12,448]{1,0:T(8,128)(2,1)}, u32[]{:S(2)}) copy-start(bf16[12,448]{1,0:T(8,128)(2,1)} %param.15) | copy-start | bytes 32260
  0.7 74.7 %collective-permute-start.2 = (bf16[512,448]{0,1:T(8,128)(2,1)}, bf16[512,448]{0,1:T(8,128)(2,1)S(1)}, u32[]{:S(2)}, u32[]{:S(2)}) collective-permute-start(bf16[512,448]{0,1:T(8,128)(2,1)} %bitcast.173), channel_id=1, source_target_pairs={{0,8},{8,0},{16,24},{24,16},{32,40},{40,32},{48,56},{56,48},{64,72... | collective-permute-start | bytes 1376264 | tf_op jit(solution)/shard_map/ppermute | solution.py:18
  15.9 18.4 %all-to-all-start.2 = ((bf16[64,2,448]{2,1,0:T(2,128)(2,1)}), bf16[64,2,448]{2,1,0:T(2,128)(2,1)S(1)}, u32[]{:S(2)}, u32[]{:S(2)}) async-start(bf16[64,2,448]{2,1,0:T(2,128)(2,1)} %select_convert_fusion.3), calls=%async_computation.2 | async-start | bytes 262144 | tf_op jit(solution)/shard_map/all_to_all | solution.py:67
  24.0 101.0 %collective-permute-start.1 = (bf16[64,3584]{1,0:T(8,128)(2,1)}, bf16[64,3584]{1,0:T(8,128)(2,1)}, u32[]{:S(2)}, u32[]{:S(2)}) collective-permute-start(bf16[64,3584]{1,0:T(8,128)(2,1)} %bitcast.6), channel_id=1, source_target_pairs={{0,8},{8,0},{16,24},{24,16},{32,40},{40,32},{48,56},{56,48},{64,72... | collective-permute-start | bytes 1376264 | tf_op jit(solution)/shard_map/ppermute | solution.py:18
  26.4 112.4 %collective-permute-start = (bf16[64,3584]{1,0:T(8,128)(2,1)}, bf16[64,3584]{1,0:T(8,128)(2,1)}, u32[]{:S(2)}, u32[]{:S(2)}) collective-permute-start(bf16[64,3584]{1,0:T(8,128)(2,1)} %bitcast.3), channel_id=1, source_target_pairs={{0,8},{8,0},{16,24},{24,16},{32,40},{40,32},{48,56},{56,48},{64,72... | collective-permute-start | bytes 1376264 | tf_op jit(solution)/shard_map/ppermute | solution.py:18
  28.4 47.0 %copy-start.16 = (bf16[1,512,448]{1,2,0:T(8,128)(2,1)S(1)}, bf16[1,512,448]{1,2,0:T(8,128)(2,1)}, u32[]{:S(2)}) copy-start(bf16[1,512,448]{1,2,0:T(8,128)(2,1)} %param.20) | copy-start | bytes 1376260
  34.4 16.7 %all-to-all-start = ((bf16[64,2,448]{2,1,0:T(2,128)(2,1)}), bf16[64,2,448]{2,1,0:T(2,128)(2,1)S(1)}, u32[]{:S(2)}, u32[]{:S(2)}) async-start(bf16[64,2,448]{2,1,0:T(2,128)(2,1)} %broadcast_select_fusion), calls=%async_computation | async-start | bytes 262144 | tf_op jit(solution)/shard_map/all_to_all | solution.py:60
  75.5 2.2 copy-start.6
  77.7 56.9 %all-to-all-start.3 = ((bf16[2,512,448]{2,0,1:T(2,128)(2,1)}), bf16[2,512,448]{2,0,1:T(2,128)(2,1)}, u32[]{:S(2)}, u32[]{:S(2)}) async-start(bf16[2,512,448]{2,0,1:T(2,128)(2,1)} %copy.67), calls=%async_computation.3 | async-start | bytes 2097152 | tf_op jit(solution)/shard_map/all_to_all | solution.py:120
  134.5 22.2 %all-to-all-start.6 = ((bf16[8,2,28672]{2,1,0:T(2,128)(2,1)}), bf16[8,2,28672]{2,1,0:T(2,128)(2,1)}, u32[]{:S(2)}, u32[]{:S(2)}) async-start(bf16[8,2,28672]{2,1,0:T(2,128)(2,1)} %reshape.373), calls=%async_computation.6 | async-start | bytes 1835008 | tf_op jit(solution)/shard_map/all_to_all | solution.py:134
  151.9 4.0 %copy-start.10 = (bf16[1,64,3584]{2,1,0:T(8,128)(2,1)S(1)}, bf16[1,64,3584]{2,1,0:T(8,128)(2,1)}, u32[]{:S(2)}) copy-start(bf16[1,64,3584]{2,1,0:T(8,128)(2,1)} %copy-done.9) | copy-start | bytes 1376260
  156.8 70.6 %all-to-all-start.5 = ((bf16[8,2,28672]{2,1,0:T(2,128)(2,1)}), bf16[8,2,28672]{2,1,0:T(2,128)(2,1)}, u32[]{:S(2)}, u32[]{:S(2)}) async-start(bf16[8,2,28672]{2,1,0:T(2,128)(2,1)} %reshape.375), calls=%async_computation.5 | async-start | bytes 1835008 | tf_op jit(solution)/shard_map/all_to_all | solution.py:133
  209.9 90.2 %collective-permute-start.3 = (bf16[64,3584]{1,0:T(8,128)(2,1)}, bf16[64,3584]{1,0:T(8,128)(2,1)}, u32[]{:S(2)}, u32[]{:S(2)}) collective-permute-start(bf16[64,3584]{1,0:T(8,128)(2,1)} %select_convert_fusion.2), channel_id=1, source_target_pairs={{0,8},{8,0},{16,24},{24,16},{32,40},{40,32},{48,56},{56,48},{64,72... | collective-permute-start | bytes 1376264 | tf_op jit(solution)/shard_map/ppermute | solution.py:18
  222.9 9.4 %copy-start.14 = (bf16[128,2,512]{0,2,1:T(8,128)(2,1)S(1)}, bf16[128,2,512]{0,2,1:T(8,128)(2,1)}, u32[]{:S(2)}) copy-start(bf16[128,2,512]{0,2,1:T(8,128)(2,1)} %copy-done.13) | copy-start | bytes 786436
  225.5 76.7 %collective-permute-start.4 = (bf16[64,3584]{1,0:T(8,128)(2,1)}, bf16[64,3584]{1,0:T(8,128)(2,1)}, u32[]{:S(2)}, u32[]{:S(2)}) collective-permute-start(bf16[64,3584]{1,0:T(8,128)(2,1)} %select_convert_fusion.1), channel_id=1, source_target_pairs={{0,8},{8,0},{16,24},{24,16},{32,40},{40,32},{48,56},{56,48},{64,72... | collective-permute-start | bytes 1376264 | tf_op jit(solution)/shard_map/ppermute | solution.py:18
  227.4 15.3 %all-to-all-start.1 = ((bf16[64,2,448]{2,1,0:T(2,128)(2,1)}), bf16[64,2,448]{2,1,0:T(2,128)(2,1)S(1)}, u32[]{:S(2)}, u32[]{:S(2)}) async-start(bf16[64,2,448]{2,1,0:T(2,128)(2,1)} %reshape.220), calls=%async_computation.1 | async-start | bytes 262144 | tf_op jit(solution)/shard_map/all_to_all | solution.py:107
  232.3 41.3 %copy-start.5 = (bf16[2,64,8,448]{3,1,2,0:T(8,128)(2,1)S(1)}, bf16[2,64,8,448]{3,1,2,0:T(8,128)(2,1)}, u32[]{:S(2)}) copy-start(bf16[2,64,8,448]{3,1,2,0:T(8,128)(2,1)} %copy.76) | copy-start | bytes 2752516
  242.7 30.9 %copy-start.15 = (bf16[64,2,448]{2,1,0:T(2,128)(2,1)}, bf16[64,2,448]{2,1,0:T(2,128)(2,1)S(1)}, u32[]{:S(2)}) copy-start(bf16[64,2,448]{2,1,0:T(2,128)(2,1)S(1)} %all-to-all-done.1) | copy-start | bytes 344068
  243.4 44.8 %all-to-all-start.4 = ((bf16[8,128,2,64]{1,3,2,0:T(8,128)(2,1)}), bf16[8,128,2,64]{1,3,2,0:T(8,128)(2,1)S(1)}, u32[]{:S(2)}, u32[]{:S(2)}) async-start(bf16[8,128,2,64]{1,3,2,0:T(8,128)(2,1)} %stack.47), calls=%async_computation.4 | async-start | bytes 524288 | tf_op jit(solution)/shard_map/all_to_all | solution.py:7
  250.6 53.6 %collective-permute-start.5 = (bf16[512,448]{0,1:T(8,128)(2,1)}, bf16[512,448]{0,1:T(8,128)(2,1)}, u32[]{:S(2)}, u32[]{:S(2)}) collective-permute-start(bf16[512,448]{0,1:T(8,128)(2,1)} %select_convert_fusion), channel_id=1, source_target_pairs={{0,8},{8,0},{16,24},{24,16},{32,40},{40,32},{48,56},{56,48},{64,72... | collective-permute-start | bytes 1376264 | tf_op jit(solution)/shard_map/ppermute | solution.py:18
  279.4 7.2 %copy-start.18 = (f32[12,8]{1,0:T(8,128)S(1)}, f32[12,8]{1,0:T(8,128)}, u32[]{:S(2)}) copy-start(f32[12,8]{1,0:T(8,128)} %copy-done.17) | copy-start | bytes 1156
  289.6 20.9 %all-to-all-start.7 = ((bf16[64,2,448]{2,1,0:T(2,128)(2,1)}), bf16[64,2,448]{2,1,0:T(2,128)(2,1)S(1)}, u32[]{:S(2)}, u32[]{:S(2)}) async-start(bf16[64,2,448]{2,1,0:T(2,128)(2,1)} %reshape.226), calls=%async_computation.7 | async-start | bytes 262144 | tf_op jit(solution)/shard_map/all_to_all | solution.py:142
  (10 other events, 12.0 us)
